TPU v7x, 32 devices: a whole 2x2x4 slice. The times are simulated.
32 devices in a mesh: dp: 8 (over z, y), tp: 4 (over x, core).
Axes of the slice: x: 2, y: 2, z: 4, core: 2. Of those that a mesh axis runs over, the one named last changes fastest.
Arguments:
- inputs: bfloat16 [1024, 16, 768], P('tp', 'dp'), may hold values from -6 to 6
- lengths: int32 [16], P('dp'), may hold values from 256 to 1024, as said below
- w_query: bfloat16 [768, 768], P(None, 'tp'), may hold values from -0.21875 to 0.21875
- b_query: float32 [768], P('tp'), may hold values from -3 to 3
- w_key: bfloat16 [768, 768], P(None, 'tp'), may hold values from -0.21875 to 0.21875
- w_value: bfloat16 [768, 768], P(None, 'tp'), may hold values from -0.21875 to 0.21875
- b_value: float32 [768], P('tp'), may hold values from -0.2 to 0.2
- w_out: bfloat16 [768, 768], P('tp'), may hold values from -6 to 6
- b_out: float32 [768], replicated, may hold values from -3 to 3
- norm1_gain: float32 [768], replicated, may hold values from 0.5 to 1.5
- norm1_bias: float32 [768], replicated, may hold values from -2 to 2
- w_up: bfloat16 [768, 3072], P(None, 'tp'), may hold values from -0.21875 to 0.21875
- b_up: float32 [3072], P('tp'), may hold values from -3 to 3
- w_down: bfloat16 [3072, 768], P('tp'), may hold values from -0.109375 to 0.109375
- b_down: float32 [768], replicated, may hold values from -3 to 3
- norm2_gain: float32 [768], replicated, may hold values from 0.5 to 1.5
- norm2_bias: float32 [768], replicated, may hold values from -2 to 2
- cotangent: bfloat16 [1024, 16, 768], P('tp', 'dp'), may hold values from -6 to 6
Outputs:
- outputs: bfloat16 [1024, 16, 768], P('tp', 'dp')
- input_grad: float32 [1024, 16, 768], P('tp', 'dp')
- grad_w_query: float32 [768, 768], P(None, 'tp')
- grad_b_query: float32 [768], P('tp')
- grad_w_key: float32 [768, 768], P(None, 'tp')
- grad_w_value: float32 [768, 768], P(None, 'tp')
- grad_b_value: float32 [768], P('tp')
- grad_w_out: float32 [768, 768], P('tp')
- grad_b_out: float32 [768], replicated
- grad_norm1_gain: float32 [768], replicated
- grad_norm1_bias: float32 [768], replicated
- grad_w_up: float32 [768, 3072], P(None, 'tp')
- grad_b_up: float32 [3072], P('tp')
- grad_w_down: float32 [3072, 768], P('tp')
- grad_b_down: float32 [768], replicated
- grad_norm2_gain: float32 [768], replicated
- grad_norm2_bias: float32 [768], replicated
Inputs may be any that keep to these rules, and one draw needn't show every extreme that they name: Utterance b occupies its first lengths[b] slots; the rest are padding. Utterance 0 has exactly 1024 valid frames.
All inputs are finite; a program needn't handle non-finite values.
Results may differ from a plain program's by a relative error of at most 0.018.
Values may be sent and summed in bfloat16 or wider, within the bound.
A program may use at most 128 MiB of HBM per device.

v0:
```python
import functools
import math

import jax
import jax.numpy as jnp
from jax import lax
from jax.experimental import pallas as pl
from jax.experimental.pallas import tpu as pltpu
from jax.sharding import PartitionSpec as P

HEAD_DIM = 64
EPS = 1e-05
ROOT_HALF = 0.7071067811865476
DENSITY = 0.3989422804014327
SCALE = 0.125
NEG = -1e30
F32 = jnp.float32
BF16 = jnp.bfloat16


def dn(a, b):
    return lax.dot_general(a, b, (((1,), (0,)), ((), ())), preferred_element_type=F32)


def dnt(a, b):
    return lax.dot_general(a, b, (((1,), (1,)), ((), ())), preferred_element_type=F32)


def dtn(a, b):
    return lax.dot_general(a, b, (((0,), (0,)), ((), ())), preferred_element_type=F32)


def split3(v):
    hi = v.astype(BF16).astype(F32)
    rest = v - hi
    mid = rest.astype(BF16).astype(F32)
    return hi, mid, rest - mid


def mean(v):
    return jnp.mean(v, -1, keepdims=True)


def col_sum(v):
    return jnp.sum(v, 0, keepdims=True)


def chunk_of(n):
    for c in (96, 64, 48, 32, 16):
        if n % c == 0:
            return c
    return n


ORDERS = {
    ('down', 0): [0, 1, 2, 'x'],
    ('down', 1): [1, 0, 'x', 2],
    ('down', 2): [1, 0, 'x', 2],
    ('down', 3): ['x', 0, 1, 2],
    ('up', 0): [0, 1, 'x', 2],
    ('up', 1): [0, 'x', 1, 2],
    ('up', 2): ['x', 0, 1, 2],
    ('up', 3): ['x', 0, 1, 2],
    ('attn', 0): ['x', 0, 1, 2],
    ('attn', 1): ['x', 0, 1, 2],
    ('attn', 2): ['x', 0, 1, 2],
    ('attn', 3): [1, 0, 'x', 2],
}
SCHEDULE = {
    'hidden0': [('down', 1), ('down', 0)],
    'hidden1': [('down', 3)],
    'ctx0': [('up', 0), ('down', 2)],
    'ctx1': [('down', 0), ('up', 2)],
    ('head', 'o', 0): [('up', 0), ('up', 1)],
    ('head', 'o', 1): [('up', 0), ('up', 3), ('down', 1), ('down', 3), ('down', 0)],
    ('head', 'o', 2): [('down', 2), ('up', 1), ('down', 1), ('attn', 3)],
    ('qk', 'o'): [('up', 0), ('down', 3), ('down', 2), ('up', 2), ('down', 0), ('up', 1)],
    ('head', 's', 0): [('up', 0), ('up', 3), ('down', 1)],
    ('head', 's', 1): [('down', 3), ('attn', 3)],
    ('head', 's', 2): [('up', 0), ('down', 2), ('up', 2), ('down', 1), ('down', 0)],
    ('qk', 's'): [('up', 3), ('attn', 1), ('up', 1), ('down', 2), ('down', 3), ('attn', 0)],
    'dx0': [('up', 2), ('down', 0)],
    'dx1': [('attn', 1), ('up', 3), ('attn', 2), ('down', 1), ('attn', 3), ('up', 1), 'sums'],
    "tail": [('down', 3), ('down', 2), ('attn', 0), ('up', 2), ('attn', 1), ('attn', 2), ('up', 3), 'sums', ('attn', 3), ('up', 1), ('attn', 0), ('attn', 1), ('up', 2), ('attn', 2), ('attn', 0), ('up', 3), ('attn', 1), 'sums', ('attn', 2), ('attn', 3), ('attn', 0), 'sums', ('attn', 1), ('attn', 2), ('attn', 0), ('attn', 3), 'sums', ('attn', 2)],
}


class Plan:
    def __init__(self, block, width, head_cols, ff_local, dp):
        self.block = block
        self.slots = 4 * block
        self.own = 2 * block
        self.width = width
        self.head_cols = head_cols
        self.heads = head_cols // HEAD_DIM
        self.ff = ff_local
        self.dp = dp
        self.bits = dp.bit_length() - 1
        self.wide = max(width, ff_local, -(-3 * head_cols // 128) * 128)
        self.qkv_cols = -(-3 * head_cols // 128) * 128
        self.out_cols = -(-head_cols // 128) * 128
        self.streams = {}
        for name, rows in (("down", ff_local), ("up", width), ("attn", 4 * head_cols)):
            for k in range(4):
                n = rows // 4
                self.streams[(name, k)] = (name, k * n, n, self.order((name, k)))

    def order(self, key):
        order = [d for d in ORDERS[key] if d == "x" or d < self.bits]
        return order + list(range(3, self.bits))

    def steps(self, n, order):
        steps, both = [], 2
        for k, dim in enumerate(order):
            if dim == "x":
                both = 1
                steps.append((dim, both, n, False))
                continue
            last = both == 1 and k == len(order) - 1
            halve = not last and (n // 2) % 16 == 0
            if halve:
                n //= 2
            steps.append((dim, both, n, halve))
        return steps


    def x_first(self, key):
        return self.streams[key][3][0] == "x"

    def moves(self):
        events = []

        def point(name, *keys, tags="os"):
            events.append((name, [k for k in keys if ("o" if self.x_first(k) else "s") in tags]))

        for name in ("down", "up"):
            for j in range(2):
                for tag in "os":
                    point((name, tag, j), (name, 2 * j), (name, 2 * j + 1), tags=tag)
            if name == "down":
                point("slope")
        for name in ("hidden0", "hidden1", "ctx0", "ctx1"):
            point(name)
        point("gout", ("attn", 3))
        for tag in "os":
            for h in range(self.heads):
                point(("head", tag, h))
            point(("qk", tag), ("attn", 0), ("attn", 1), tags=tag)
            point(("v", tag), ("attn", 2), tags=tag)
        events += [("dx0", ["sums"]), ("dx1", []), ("tail", [])]
        total = {"sums": 3 + self.bits}
        for key, (_, _, n, order) in self.streams.items():
            steps = self.steps(n, order)
            total[key] = 1 + len(steps) + sum(halve for _, _, _, halve in steps)
        at, moves = {}, {}
        for name, begun in events:
            moves[name] = [(key, 0) for key in begun]
            at.update({key: 1 for key in begun})
            for key in SCHEDULE.get(name, ()):
                if key in at and at[key] < total[key]:
                    moves[name].append((key, at[key]))
                    at[key] += 1
        while any(at[key] < total[key] for key in at):
            for key in at:
                if at[key] < total[key]:
                    moves["tail"].append((key, at[key]))
                    at[key] += 1
        return moves


def layer(plan, names, *refs):
    r = dict(zip(names, refs))
    block, slots, own, width = plan.block, plan.slots, plan.own, plan.width
    hc, heads, ff, dpn, bits = plan.head_cols, plan.heads, plan.ff, plan.dp, plan.bits
    dp = lax.axis_index("dp")
    tp = lax.axis_index("tp")
    x = lax.div(tp, 2)
    c = lax.rem(tp, 2)
    ox = 1 - x
    bit = [lax.rem(lax.div(dp, 1 << b), 2) for b in range(bits)]
    part = {b: (dp + (1 << b) * (1 - 2 * bit[b]), tp) for b in range(bits)}
    part["x"] = (dp, lax.rem(tp + 2, 4))
    part["c"] = (dp, tp + 1 - 2 * c)
    mesh_id = pl.DeviceIdType.MESH

    ssem, rsem, lsem = r["ssem"], r["rsem"], r["lsem"]
    count = {"r": 0, "l": 0}
    pending = []

    def take(n):
        count["r"] += n
        return count["r"] - n

    def remote(src, dst, i, who):
        return pltpu.make_async_remote_copy(
            src_ref=src,
            dst_ref=dst,
            send_sem=ssem.at[i],
            recv_sem=rsem.at[i],
            device_id=part[who],
            device_id_type=mesh_id,
        )

    def prepare(src, dst, who, keep=True):
        copy = remote(src, dst, take(1), who)
        if keep:
            pending.append(copy)
        return copy

    def send(src, dst, who):
        copy = prepare(src, dst, who)
        copy.start()
        return copy

    def local_prepare(src, dst):
        i = count["l"]
        count["l"] += 1
        return pltpu.make_async_copy(src, dst, lsem.at[i])

    def local(src, dst):
        copy = local_prepare(src, dst)
        copy.start()
        return copy

    def mult(v, m=16):
        return pl.multiple_of(v, math.gcd(m, 128))

    def row(i):
        return pl.multiple_of(lax.rem(c * own + i * block, slots), block)

    own0 = pl.multiple_of(c * own, own)
    mine = pl.multiple_of(x * block, block)
    other = pl.multiple_of(ox * block, block)

    xs = r["X"]
    local_a = []
    for k, name in enumerate(("wq", "wk", "wv", "wo")):
        local_a.append(local(r[name], r["Wwa"].at[x, pl.ds(k * hc, hc)]))
    local_x = local(r["inputs"], r["XI"])
    local_c = local(r["cot"], r["CI"])
    vectors = ("bq", "bv", "bu", "bo", "g1", "c1", "bd", "g2", "c2")
    local_v = [local(r[n], r["V" + n]) for n in vectors]
    barrier = pltpu.get_barrier_semaphore()
    for who in part.values():
        pl.semaphore_signal(barrier, inc=1, device_id=who, device_id_type=mesh_id)
    pl.semaphore_wait(barrier, len(part))

    gbits = min(2, bits)
    parts = 1 << gbits
    piece = lax.rem(dp, parts)

    def cut(name, k, of):
        if name == "wa":
            return k * hc, hc // parts, hc // parts
        n = r[name].shape[0] // parts
        return k * n // of, n // of, n

    def weight_x(name, k, of):
        start, size, step_rows = cut(name, k, of)
        src = r[("wq", "wk", "wv", "wo")[k]] if name == "wa" else r[name]
        off = mult(piece * step_rows, 16)
        from_at = pl.ds(off if name == "wa" else mult(off + start, 16), size)
        return send(src.at[from_at], r["W" + name].at[x, pl.ds(mult(off + start, 16), size)], "x")

    def weight_hop(name, k, of):
        start, size, step_rows = cut(name, k, of)
        at = pl.ds(mult(piece * step_rows + start, 16), size)
        dst = r["W" + name].at[ox, at]
        return [prepare(dst, dst, b) for b in range(gbits)]

    def weight_far(name, k, of):
        if gbits < 2:
            return []
        start, size, step_rows = cut(name, k, of)
        b = k % 2
        o = 1 - b
        from_piece = piece + (1 << o) * (1 - 2 * bit[o])
        at = pl.ds(mult(from_piece * step_rows + start, 16), size)
        dst = r["W" + name].at[ox, at]
        return [prepare(dst, dst, b)]

    def arrived(copies):
        for copy in copies:
            copy.wait_recv()

    half = block // 2
    wa_x = [weight_x("wa", k, 4) for k in range(4)]
    b_x = [send(r[n], r["O" + n], "x") for n in ("bq", "bv", "bu")]

    def divide(ref):
        even, odd = ref[:, 0, :], ref[:, 1, :]
        return jnp.where(x == 0, even, odd), jnp.where(x == 0, odd, even)

    local_x.wait()
    at_mine = pl.ds(own0 + mine, block)
    own_rows, far_rows = divide(r["XI"])
    r["XO"][...] = far_rows
    xs[at_mine, :] = own_rows
    x_x = []
    for k in range(2):
        src = r["XO"].at[pl.ds(k * half, half)]
        x_x.append(send(src, xs.at[pl.ds(own0 + mine + k * half, half)], "x"))
    late_x = {(name, k): weight_x(name, k, 2) for name in ("wu", "wd") for k in range(2)}
    x_c = [send(xs.at[at_mine], xs.at[at_mine], "c")]
    local_c.wait()
    own_rows, far_rows = divide(r["CI"])
    r["CO"][...] = far_rows
    r["CT"][pl.ds(mine, block), :] = own_rows
    c_x = send(r["CO"], r["CT"].at[pl.ds(mine, block)], "x")
    local_w = [local(r[name], r["W" + name].at[x]) for name in ("wu", "wd")]

    bias = r["B"]
    rep = r["R"]
    lane = lax.broadcasted_iota(jnp.int32, (block, 128), 1)
    valid = r["lens"][x]
    for copy in local_v:
        copy.wait()
    for k, name in enumerate(vectors[3:]):
        rep[k : k + 1, :width] = r["V" + name][...].reshape(1, width)

    def set_bias(s, q, v, u):
        bias[s, 0:1, :] = jnp.zeros((1, plan.wide), F32)
        bias[s, 0:1, :hc] = q[...].reshape(1, hc)
        bias[s, 0:1, 2 * hc : 3 * hc] = v[...].reshape(1, hc)
        bias[s, 1:2, :ff] = u[...].reshape(1, ff)

    set_bias(x, r["Vbq"], r["Vbv"], r["Vbu"])
    def project(s, first):
        i = lax.div(first, block)
        at = pl.ds(pl.multiple_of(first, block), block)
        y = dnt(xs[at, :], r["Wwa"][s, : plan.qkv_cols, :]) + bias[s, 0:1, : plan.qkv_cols]
        slot0 = first + block * jnp.where(i == 1, 1, 0) - block * jnp.where(i == 2, 1, 0)
        slot = slot0 + lax.broadcasted_iota(jnp.int32, (block, 128), 0)
        masked = jnp.where(slot < valid, 0.0, NEG)
        real = lane < HEAD_DIM
        k_end = jnp.where(lane == 64, masked, jnp.where(lane < 68, 1.0, 0.0))
        q_end = jnp.where(lane == 64, 1.0, 0.0)
        v_end = jnp.where(lane < 67, 1.0, 0.0)
        for k, (name, end) in enumerate((("QP", q_end), ("KP", k_end), ("VP", v_end))):
            for h in range(heads):
                unit = k * heads + h
                tile = y[:, unit // 2 * 128 : unit // 2 * 128 + 128]
                if unit % 2:
                    tile = pltpu.roll(tile, 64, 1)
                if k == 0:
                    tile = tile * SCALE
                r[name][s * heads + h, at, :] = jnp.where(real, tile, end).astype(BF16)

    def started(copies):
        for copy in copies:
            copy.start()
        return copies

    def frames_at(k, offset):
        return lax.rem(own0 + k * own, slots) + offset

    for copy in local_a:
        copy.wait()
    wa_h, wa_f = [], []
    for k in range(4):
        wa_x[k].wait_recv()
        wa_h.append(started(weight_hop("wa", k, 4)))
    for k in range(4):
        arrived(wa_h[k])
        wa_f += started(weight_far("wa", k, 4))
    arrived(b_x)
    set_bias(ox, r["Obq"], r["Obv"], r["Obu"])
    x_x[0].wait_recv()
    at_other = [pl.ds(own0 + other + k * half, half) for k in range(2)]
    x_c.append(send(xs.at[at_other[0]], xs.at[at_other[0]], "c"))
    x_c.pop(0).wait_recv()
    arrived(wa_f)

    @pl.loop(0, 4)
    def _(i):
        project(lax.rem(i, 2), frames_at(lax.div(i, 2), mine))

    x_x[1].wait_recv()
    x_c.append(send(xs.at[at_other[1]], xs.at[at_other[1]], "c"))
    for k in range(2):
        if k:
            arrived(x_c)

        @pl.loop(0, 2)
        def _(s, k=k):
            project(s, frames_at(k, other))

    for copy in local_w:
        copy.wait()

    row_tiles = [slice(i * block, (i + 1) * block) for i in range(4)]

    def attend(hs):
        queries = [r["QP"][hs, at, :] for at in row_tiles]
        scores = [dnt(q, r["KP"][hs]) for q in queries]
        done = []
        for score in scores:
            top = jnp.max(score, -1, keepdims=True)
            done.append((dn(jnp.exp(score - top).astype(BF16), r["VP"][hs]), top))
        for at, q, (o, top) in zip(row_tiles, queries, done):
            total = o[:, HEAD_DIM : HEAD_DIM + 1]
            r["DC"][hs, at, :] = (o / total).astype(BF16)
            hi, mid, low = split3(-(top + jnp.log(total)))
            ends = jnp.where(lane == 66, mid, jnp.where(lane == 67, low, q.astype(F32)))
            r["QP"][hs, at, :] = jnp.where(lane == 65, hi, ends).astype(BF16)

    chunks = [(name, k) for name in ("wu", "wd") for k in range(2)]
    late_h = {key: weight_hop(*key, 2) for key in chunks}
    late_f = {key: weight_far(*key, 2) for key in chunks}

    def hop(name, k):
        late_x[name, k].wait_recv()
        started(late_h[name, k])

    def far(name, k):
        arrived(late_h[name, k])
        started(late_f[name, k])

    progress = [(1, hop, "wu", 1), (2, far, "wu", 0), (3, hop, "wd", 0)]
    progress += [(4, far, "wu", 1), (5, hop, "wd", 1)]
    hop("wu", 0)

    @pl.loop(0, 2 * heads)
    def _(i):
        attend(lax.rem(x * heads + i, 2 * heads))
        for when, move, name, k in progress:

            @pl.when(i == min(when, 2 * heads - 1))
            def _(move=move, name=name, k=k):
                move(name, k)

    def join(dst, s, parts, first, last):
        @pl.loop(first, last)
        def _(i):
            at = pl.ds(pl.multiple_of(i * block, block), block)
            for t in range(0, len(parts), 2):
                ref, h = parts[t]
                tile = ref[s * heads + h, at, :].astype(F32)
                odd = jnp.zeros_like(tile)
                if t + 1 < len(parts):
                    ref, h = parts[t + 1]
                    odd = pltpu.roll(ref[s * heads + h, at, :].astype(F32), 64, 1)
                tile = jnp.where(lane < HEAD_DIM, tile, odd)
                dst[s, at, t * 64 : t * 64 + 128] = tile.astype(BF16)

    @pl.loop(0, 2)
    def _(s):
        join(r["C"], s, [(r["DC"], h) for h in range(heads)], 0, 4)

    sbuf, rbuf = r["SB"], r["RB"]

    def exchange(partial):
        base = take(2)

        @pl.loop(0, 2)
        def _(i):
            sbuf[i] = partial(row(2 + i)).astype(BF16)
            remote(sbuf.at[i], rbuf.at[i], base + i, "c").start()

        return base

    def received(base, i):
        remote(sbuf.at[i], rbuf.at[i], base + i, "c").wait_recv()
        return rbuf[i].astype(F32)

    def left(base):
        for i in range(2):
            remote(sbuf.at[i], rbuf.at[i], base + i, "c").wait_send()

    def share(buf, base, i):
        at = pl.ds(row(i), block)
        return remote(buf.at[at], buf.at[at], base + i, "c")

    def shared(buf):
        base = take(2)
        copies = [share(buf, base, i) for i in range(2)]
        pending.extend(copies)
        return base, copies

    sums = r["sums"]
    sums[...] = jnp.zeros_like(sums)

    def add_sum(k, v, n=None):
        n = v.shape[-1]
        sums[pl.ds(k, 1), :n] = sums[pl.ds(k, 1), :n] + v

    def attn_out(at0):
        at = pl.ds(at0, block)
        return sum(dn(r["C"][s, at, :hc], r["Wwa"][s, 3 * hc :, :]) for s in range(2))

    ex = exchange(attn_out)
    hb_base, hb_c = shared(r["HB"])

    @pl.loop(0, 2)
    def _(i):
        a = attn_out(row(i)) + rep[0:1, :width]
        z = xs[pl.ds(row(i), block), :].astype(F32) + a + received(ex, i)
        z = z - mean(z)
        inv = lax.rsqrt(mean(z * z) + EPS)
        n1 = z * inv
        at = pl.ds(pl.multiple_of(i * block, block), block)
        r["N1"][at, :] = n1
        r["INV"][at, :] = jnp.broadcast_to(inv, (block, 128))
        r["HB"][pl.ds(row(i), block), :] = (n1 * rep[1:2, :width] + rep[2:3, :width]).astype(BF16)
        share(r["HB"], hb_base, i).start()
    left(ex)

    def up(s, first, last):
        @pl.loop(first, last)
        def _(i):
            at = pl.ds(row(i), block)
            u = dn(r["HB"][at, :], r["Wwu"][s]) + bias[s, 1:2, :ff]
            cdf = 0.5 * (1.0 + lax.erf(u * ROOT_HALF))
            r["G"][s, at, :] = (u * cdf).astype(BF16)
            r["SL"][s, at, :] = u.astype(BF16)

    far("wd", 0)
    up(x, 0, 2)
    arrived(hb_c)
    far("wd", 1)
    up(x, 2, 4)
    arrived(late_f["wu", 0] + late_f["wu", 1])
    up(ox, 0, 4)

    def ffn_out(at0):
        at = pl.ds(at0, block)
        return dn(r["G"][0, at, :], r["Wwd"][0]) + dn(r["G"][1, at, :], r["Wwd"][1])

    arrived(late_f["wd", 0] + late_f["wd", 1])
    ex = exchange(ffn_out)
    df_base, df_c = shared(r["DF"])
    c_x.wait_recv()

    @pl.loop(0, 2)
    def _(i):
        at = pl.ds(pl.multiple_of(i * block, block), block)
        hidden = r["N1"][at, :] * rep[1:2, :width] + rep[2:3, :width]
        f = ffn_out(row(i)) + rep[3:4, :width]
        z = hidden + f + received(ex, i)
        z = z - mean(z)
        inv = lax.rsqrt(mean(z * z) + EPS)
        n2 = z * inv
        r["OB"][at, :] = (n2 * rep[4:5, :width] + rep[5:6, :width]).astype(BF16)
        dy = r["CT"][at, :].astype(F32)
        add_sum(4, col_sum(dy * n2))
        add_sum(5, col_sum(dy))
        e2 = dy * rep[4:5, :width]
        dz = inv * (e2 - mean(e2) - n2 * mean(e2 * n2))
        r["DZ"][at, :] = dz
        df = dz.astype(BF16)
        add_sum(3, col_sum(df.astype(F32)))
        r["DF"][pl.ds(row(i), block), :] = df
        share(r["DF"], df_base, i).start()
    left(ex)
    out_x = send(r["OB"].at[pl.ds(other, block)], r["out"].at[x], "x")
    out_l = local(r["OB"].at[pl.ds(mine, block)], r["out"].at[x])

    def adder(dst, d, row0, src, sd, n):
        size = chunk_of(n)

        @pl.loop(0, n // size)
        def _(i):
            at = pl.ds(mult(row0 + i * size), size)
            got = src[sd, pl.ds(mult(i * size), size), :].astype(F32)
            dst[d, at, :] = (dst[d, at, :].astype(F32) + got).astype(BF16)

    def stream(key):
        name, row0, n, order = plan.streams[key]
        grad, final = r["G_" + name], r["F_" + name]
        both, halved, copies, then = True, [], [], []
        for k, (dim, _, n, halve) in enumerate(plan.steps(n, order)):
            got = r["S_%s_%d_%d" % (*key, k)]
            if dim == "x":
                copies.append(prepare(grad.at[ox, pl.ds(row0, n)], got.at[0], "x"))
                both = False
            else:
                sent = row0
                if halve:
                    halved.append(dim)
                    sent = mult(row0 + (1 - bit[dim]) * n)
                    row0 = mult(row0 + bit[dim] * n)
                at = pl.ds(sent, n)
                src = grad.at[:, at] if both else grad.at[x, at]
                copies.append(prepare(src, got if both else got.at[0], dim, halve))

            def add(copy=copies[-1], got=got, row0=row0, n=n, both=both, wait=dim != "x" and not halve):
                if wait:
                    copy.wait_send()
                if both:
                    adder(grad, 0, row0, got, 0, n)
                    adder(grad, 1, row0, got, 1, n)
                else:
                    adder(grad, x, row0, got, 0, n)

            then.append([add])
        keep = local_prepare(grad.at[x, pl.ds(row0, n)], final.at[pl.ds(row0, n)])
        then[-1].append(keep.start)
        src = grad.at[x, pl.ds(row0, n)]
        for dim in reversed(halved):
            at = pl.ds(row0, n)
            copies.append(prepare(src, final.at[at], dim))
            then.append([])
            row0 = mult(row0 - bit[dim] * n)
            n *= 2
            src = final.at[pl.ds(row0, n)]
        then[len(plan.steps(plan.streams[key][2], order)) if halved else -1].append(keep.wait)
        return chain(copies, then)

    def chain(copies, then):
        def move(k):
            if k:
                copies[k - 1].wait_recv()
                for act in then[k - 1]:
                    act()
            if k < len(copies):
                copies[k].start()

        return move

    def sums_stream():
        copies, then = [], []
        for k, who in enumerate(["c", "x"] + list(range(bits))):
            n = 8 if who == "c" else 16
            copy = prepare(sums.at[pl.ds(0, n)], r["SR"].at[k, pl.ds(0, n)], who, False)

            def add(copy=copy, k=k, n=n):
                copy.wait_send()
                sums[0:n, :] = sums[0:n, :] + r["SR"][k, 0:n, :]

            copies.append(copy)
            then.append([add])
        return chain(copies, then)

    movers = {key: stream(key) for key in plan.streams}
    movers["sums"] = sums_stream()
    moves = plan.moves()

    def step(name, when=None):
        if not moves[name]:
            return

        def make():
            for key, k in moves[name]:
                movers[key](k)

        if when is None:
            make()
        else:
            pl.when(when)(make)

    def slope(first, last):
        @pl.loop(first, last)
        def _(i):
            at = pl.ds(row(i), block)
            for s in range(2):
                da = dnt(r["DF"][at, :], r["Wwd"][s])
                u = r["SL"][s, at, :].astype(F32)
                cdf = 0.5 * (1.0 + lax.erf(u * ROOT_HALF))
                du = da * (cdf + u * (DENSITY * jnp.exp(-0.5 * u * u)))
                add_sum(8 + s, col_sum(du))
                r["SL"][s, at, :] = du.astype(BF16)

    def weight_grad(name, lhs, rhs):
        dst = r["G_" + name]
        n = dst.shape[1] // 2

        @pl.loop(0, 4)
        def _(q):
            s, j = lax.rem(ox + q, 2), lax.div(q, 2)
            at = pl.ds(pl.multiple_of(j * n, n), n)
            dst[s, at, :] = dtn(lhs(s, at), rhs(s)).astype(BF16)
            for k in range(4):
                step((name, "os"[k % 2], k // 2), q == k)

    slope(0, 2)
    arrived(df_c)
    weight_grad("down", lambda s, at: r["G"][s, :, at], lambda s: r["DF"][...])
    slope(2, 4)
    step("slope")
    weight_grad("up", lambda s, at: r["HB"][:, at], lambda s: r["SL"][s])

    def hidden_back(at0):
        at = pl.ds(at0, block)
        return dnt(r["SL"][0, at, :], r["Wwu"][0]) + dnt(r["SL"][1, at, :], r["Wwu"][1])

    ex = exchange(hidden_back)
    da_base, da_c = shared(r["DA"])
    step("hidden0")

    @pl.loop(0, 2)
    def _(i):
        at = pl.ds(pl.multiple_of(i * block, block), block)
        dh = r["DZ"][at, :] + hidden_back(row(i))
        dh = dh + received(ex, i)
        n1 = r["N1"][at, :]
        add_sum(1, col_sum(dh * n1))
        add_sum(2, col_sum(dh))
        e1 = dh * rep[1:2, :width]
        dz = r["INV"][at, 0:1] * (e1 - mean(e1) - n1 * mean(e1 * n1))
        r["DZ"][at, :] = dz
        da = dz.astype(BF16)
        add_sum(0, col_sum(da.astype(F32)))
        r["DA"][pl.ds(row(i), block), :] = da
        share(r["DA"], da_base, i).start()
    left(ex)
    step("hidden1")

    rows_e = lax.broadcasted_iota(jnp.int32, (hc, heads * 128), 0)
    lanes_e = lax.broadcasted_iota(jnp.int32, (hc, heads * 128), 1)
    spot = lanes_e - lax.div(rows_e, HEAD_DIM) * 128
    r["E"][...] = jnp.where((spot >= 64) & (spot < 67), -1.0, 0.0).astype(BF16)

    def context_back(first, last):
        @pl.loop(first, last)
        def _(i):
            at = pl.ds(row(i), block)
            for s in range(2):
                dc = dnt(r["DA"][at, :], r["Wwa"][s, 3 * hc :, :]).astype(BF16).astype(F32)
                prod = dc * r["C"][s, at, :hc].astype(F32)
                prod_hi = prod.astype(BF16)
                prod_lo = (prod - prod_hi.astype(F32)).astype(BF16)
                ends = dn(prod_hi, r["E"][...]) + dn(prod_lo, r["E"][...])
                for h in range(heads):
                    end = ends[:, h * 128 : h * 128 + 128]
                    if 2 * h + 2 <= 2 * heads - heads % 2:
                        tile = dc[:, h // 2 * 128 : h // 2 * 128 + 128]
                        if h % 2:
                            tile = pltpu.roll(tile, 64, 1)
                    else:
                        tile = jnp.concatenate([dc[:, h * 64 :], end[:, 64:]], 1)
                    tile = jnp.where(lane < 64, tile, end)
                    hi, mid, low = split3(tile)
                    tile = jnp.where(lane == 65, mid, jnp.where(lane == 66, low, hi))
                    r["DC"][s * heads + h, at, :] = tile.astype(BF16)

    context_back(0, 2)
    step("ctx0")
    arrived(da_c)
    context_back(2, 4)
    step("ctx1")
    @pl.loop(0, 2)
    def _(s):
        r["G_attn"][s, 3 * hc :, :] = dtn(r["C"][s], r["DA"][...])[:hc].astype(BF16)

    step("gout")

    def head_back(hs):
        keys, values = r["KP"].at[hs], r["VP"].at[hs]
        r["KT"][...] = keys[...].T
        queries = [r["QP"][hs, at, :] for at in row_tiles]
        tangents = [r["DC"][hs, at, :] for at in row_tiles]
        scores = [dnt(keys[...], q) for q in queries]
        centred = [dnt(values[...], dc) for dc in tangents]
        dk = dv = 0.0
        dq = []
        for q, dc, score, middle in zip(queries, tangents, scores, centred):
            p = jnp.exp(score)
            ds = (p * middle).astype(BF16)
            dv = dv + dn(p.astype(BF16), dc)
            dk = dk + dn(ds, q)
            dq.append(dn(r["KT"][...], ds).T)
        for at, d in zip(row_tiles, dq):
            r["QP"][hs, at, :] = (d * SCALE).astype(BF16)
        r["KP"][hs] = dk.astype(BF16)
        r["VP"][hs] = dv.astype(BF16)

    g_attn = r["G_attn"]

    @pl.loop(0, 2)
    def _(i):
        s = lax.rem(ox + i, 2)

        @pl.loop(0, heads)
        def _(h):
            head_back(s * heads + h)
            for k in range(2 * heads):
                step(("head", "os"[k // heads], k % heads), i * heads + h == k)

        join(r["D3"], s, [(r[n], h) for n in ("QP", "KP", "VP") for h in range(heads)], 0, 4)
        add_sum(10 + s, col_sum(r["D3"][s].astype(F32)))
        g_attn[s, : 2 * hc, :] = dtn(r["D3"][s, :, : 2 * hc], xs[...]).astype(BF16)
        for k in range(2):
            step(("qk", "os"[k]), i == k)
        grad_v = dtn(r["D3"][s, :, 2 * hc :], xs[...])
        g_attn[s, 2 * hc : 3 * hc, :] = grad_v[:hc].astype(BF16)
        for k in range(2):
            step(("v", "os"[k]), i == k)

    def input_back(at0):
        at = pl.ds(at0, block)
        return sum(dn(r["D3"][s, at, :], r["Wwa"][s, : plan.qkv_cols, :]) for s in range(2))

    ex = exchange(input_back)
    step("dx0")

    @pl.loop(0, 2)
    def _(i):
        at = pl.ds(pl.multiple_of(i * block, block), block)
        dx = r["DZ"][at, :] + input_back(row(i))
        r["DZ"][at, :] = dx + received(ex, i)

    left(ex)
    r["DXS"][...] = r["DZ"][pl.ds(other, block), :].astype(BF16)
    dx_x = send(r["DXS"], r["dx_far"], "x")
    dx_l = local(r["DZ"].at[pl.ds(mine, block)], r["dx_own"])

    step("dx1")
    step("tail")
    r["vec"][...] = sums[...]
    out_x.wait_recv()
    dx_x.wait_recv()
    out_l.wait()
    dx_l.wait()
    for copy in pending:
        copy.wait_send()


def finish(names, *refs):
    r = dict(zip(names, refs))
    sem = r["sem"]
    used = []

    def copy(src, dst):
        made = pltpu.make_async_copy(src, dst, sem.at[len(used)])
        made.start()
        used.append(made)
        return made

    first = lax.axis_index("tp") < 2
    hc = r["g_query"].shape[0]
    targets = {"F_down": ["g_down"], "F_up": ["g_up"]}
    targets["F_attn"] = ["g_query", "g_key", "g_value", "g_out"]
    got = {}
    for n in targets:
        rows = r[n].shape[0] // 4
        for k in range(4):
            at = pl.ds(k * rows, rows)
            got[n, k] = copy(r[n].at[at], r["i_" + n].at[at])
    for n in ("dx_own", "dx_far", "out", "vec"):
        got[n] = copy(r[n], r["i_" + n])
    loads = len(used)
    for n, outs in targets.items():
        rows = r[n].shape[0] // 4
        if len(outs) > 1:
            for k in range(4):
                got[n, k].wait()
        for k in range(4):
            at = pl.ds(k * rows, rows)
            if len(outs) == 1:
                got[n, k].wait()
            r["o_" + n][at, :] = r["i_" + n][at, :].astype(F32)
            target = r[outs[k]] if len(outs) > 1 else r[outs[0]].at[at]
            copy(r["o_" + n].at[at], target)
    got["dx_own"].wait()
    got["dx_far"].wait()
    own, far = r["i_dx_own"][...], r["i_dx_far"][...].astype(F32)
    r["o_dx"][:, 0, :] = jnp.where(first, own, far)
    r["o_dx"][:, 1, :] = jnp.where(first, far, own)
    copy(r["o_dx"], r["dx"])
    got["out"].wait()
    for k in range(2):
        r["o_rows"][:, k, :] = r["i_out"][k]
    copy(r["o_rows"], r["rows"])
    got["vec"].wait()
    vec = r["i_vec"]
    width = r["s_bo"].shape[0]
    for k, n in enumerate(("bo", "g1", "c1", "bd", "g2", "c2")):
        r["s_" + n][...] = vec[k, :width]
    ff = r["s_bu"].shape[0]
    r["s_bu"][...] = jnp.where(first, vec[8, :ff], vec[9, :ff])
    b3 = jnp.where(first, vec[10:11, :], vec[11:12, :])
    r["s_bq"][...] = b3[:, :hc].reshape(hc)
    r["s_bv"][...] = b3[:, 2 * hc : 3 * hc].reshape(hc)
    for made in used[loads:]:
        made.wait()


def local(
    inputs,
    lengths,
    w_query,
    b_query,
    w_key,
    w_value,
    b_value,
    w_out,
    b_out,
    norm1_gain,
    norm1_bias,
    w_up,
    b_up,
    w_down,
    b_down,
    norm2_gain,
    norm2_bias,
    cotangent,
):
    block, utts, width = inputs.shape
    dpn = lax.axis_size("dp")
    plan = Plan(block, width, w_query.shape[1], w_up.shape[1], dpn)
    hc, ff, wide = plan.head_cols, plan.ff, plan.wide
    slots, own, heads = plan.slots, plan.own, plan.heads


    operands = [
        ("inputs", inputs),
        ("cot", cotangent),
        ("lens", lengths),
        ("wq", w_query.T),
        ("wk", w_key.T),
        ("wv", w_value.T),
        ("wo", w_out),
        ("wu", w_up),
        ("wd", w_down),
        ("bq", b_query),
        ("bv", b_value),
        ("bu", b_up),
        ("bo", b_out),
        ("g1", norm1_gain),
        ("c1", norm1_bias),
        ("bd", b_down),
        ("g2", norm2_gain),
        ("c2", norm2_bias),
    ]
    shape_of = jax.ShapeDtypeStruct
    hbm = pl.BlockSpec(memory_space=pl.ANY)
    vmem = pl.BlockSpec(memory_space=pltpu.VMEM)
    smem = pl.BlockSpec(memory_space=pltpu.SMEM)
    outs = [
        ("out", shape_of((2, block, width), BF16), hbm),
        ("dx_own", shape_of((block, width), F32), hbm),
        ("dx_far", shape_of((block, width), BF16), hbm),
        ("vec", shape_of((16, wide), F32), vmem),
    ]
    grads = (
        ("down", ff, width),
        ("up", width, ff),
        ("attn", 4 * hc, width),
    )
    for name, rows, cols in grads:
        outs.append(("F_" + name, shape_of((rows, cols), BF16), hbm))

    def v(name, shape, dtype=BF16):
        return (name, pltpu.VMEM(shape, dtype))

    scratch = [
        v("X", (slots, width)),
        v("Wwa", (2, 4 * hc, width)),
        v("Wwu", (2, width, ff)),
        v("Wwd", (2, ff, width)),
        v("B", (2, 8, wide), F32),
        *(v("V" + n, a.shape, F32) for n, a in operands[-9:]),
        v("Obq", (hc,), F32),
        v("Obv", (hc,), F32),
        v("Obu", (ff,), F32),
        v("R", (8, wide), F32),
        v("XI", (block, utts, width)),
        v("CI", (block, utts, width)),
        v("XO", (block, width)),
        v("CO", (block, width)),
        v("CT", (own, width)),
        v("QP", (2 * heads, slots, 128)),
        v("KP", (2 * heads, slots, 128)),
        v("VP", (2 * heads, slots, 128)),
        v("DC", (2 * heads, slots, 128)),
        v("C", (2, slots, plan.out_cols)),
        v("E", (hc, heads * 128)),
        v("SB", (2, block, width)),
        v("RB", (2, block, width)),
        v("N1", (own, width), F32),
        v("INV", (own, 128), F32),
        v("HB", (slots, width)),
        v("G", (2, slots, ff)),
        v("SL", (2, slots, ff)),
        v("OB", (own, width)),
        v("DZ", (own, width), F32),
        v("DF", (slots, width)),
        v("DA", (slots, width)),
        v("D3", (2, slots, plan.qkv_cols)),
        v("KT", (128, slots)),
        v("DXS", (block, width)),
        v("sums", (16, wide), F32),
        v("SR", (2 + plan.bits, 16, wide), F32),
    ]
    for name, rows, cols in grads:
        scratch.append(v("G_" + name, (2, rows, cols)))
    widths = {name: cols for name, _, cols in grads}
    for key, (name, _, rows, order) in plan.streams.items():
        for k, (_, both, n, _) in enumerate(plan.steps(rows, order)):
            scratch.append(v("S_%s_%d_%d" % (*key, k), (both, n, widths[name])))
    scratch += [
        ("ssem", pltpu.SemaphoreType.DMA((192,))),
        ("rsem", pltpu.SemaphoreType.DMA((192,))),
        ("lsem", pltpu.SemaphoreType.DMA((48,))),
    ]
    names = [n for n, _ in operands] + [n for n, _, _ in outs] + [n for n, _ in scratch]
    results = pl.pallas_call(
        functools.partial(layer, plan, names),
        out_shape=[s for _, s, _ in outs],
        in_specs=[smem if n == "lens" else hbm for n, _ in operands],
        out_specs=[s for _, _, s in outs],
        scratch_shapes=[s for _, s in scratch],
        compiler_params=pltpu.CompilerParams(
            collective_id=0, has_side_effects=True, vmem_limit_bytes=63 * 2**20
        ),
        name="encoder_layer",
    )(*[a for _, a in operands])
    got = dict(zip([n for n, _, _ in outs], results))
    inner = [got[n] for n in ("out", "dx_own", "dx_far", "F_down", "F_up", "F_attn", "vec")]
    inner_names = ["out", "dx_own", "dx_far", "F_down", "F_up", "F_attn", "vec"]
    frames = (block, utts, width)
    final = [("g_down", (ff, width), F32), ("g_up", (width, ff), F32)]
    final += [("dx", frames, F32), ("rows", frames, BF16)]
    final += [(n, (hc, width), F32) for n in ("g_query", "g_key", "g_value", "g_out")]
    small = [("s_" + n, (width,)) for n in ("bo", "g1", "c1", "bd", "g2", "c2")]
    small += [("s_bu", (ff,)), ("s_bq", (hc,)), ("s_bv", (hc,))]
    buffers = [("i_" + n, a.shape, a.dtype) for n, a in zip(inner_names, inner)]
    buffers += [("o_rows", frames, BF16), ("o_dx", frames, F32)]
    buffers += [("o_" + n, got[n].shape, F32) for n in ("F_down", "F_up", "F_attn")]
    labels = inner_names + [n for n, _, _ in final] + [n for n, _ in small]
    labels += [n for n, _, _ in buffers] + ["sem"]
    results = pl.pallas_call(
        functools.partial(finish, labels),
        in_specs=[hbm] * len(inner),
        out_specs=[hbm] * len(final) + [vmem] * len(small),
        out_shape=[shape_of(n, t) for _, n, t in final] + [shape_of(n, F32) for _, n in small],
        scratch_shapes=[pltpu.VMEM(n, t) for _, n, t in buffers]
        + [pltpu.SemaphoreType.DMA((32,))],
        compiler_params=pltpu.CompilerParams(vmem_limit_bytes=60 * 2**20),
        name="finish",
    )(*inner)
    g_down, g_up, input_grad, outputs, g_query, g_key, g_value, g_out = results[:8]
    g_bo, g_g1, g_c1, g_bd, g_g2, g_c2, g_bu, g_bq, g_bv = results[8:]
    return (
        outputs,
        input_grad,
        g_query.T,
        g_bq,
        g_key.T,
        g_value.T,
        g_bv,
        g_out,
        g_bo,
        g_g1,
        g_c1,
        g_up,
        g_bu,
        g_down,
        g_bd,
        g_g2,
        g_c2,
    )


def solution(mesh):
    whole = P()
    rows = P("tp", "dp", None)
    cols = P(None, "tp")
    down = P("tp", None)
    shard = P("tp")
    return jax.shard_map(
        local,
        mesh=mesh,
        in_specs=(
            rows,
            P("dp"),
            cols,
            shard,
            cols,
            cols,
            shard,
            down,
            whole,
            whole,
            whole,
            cols,
            shard,
            down,
            whole,
            whole,
            whole,
            rows,
        ),
        out_specs=(
            rows,
            rows,
            cols,
            shard,
            cols,
            cols,
            shard,
            down,
            whole,
            whole,
            whole,
            cols,
            shard,
            down,
            whole,
            whole,
            whole,
        ),
        check_vma=False,
    )
```

profile of v0, /device:TPU:0, one launch (start us, length us, event | category | flops | bytes accessed | tf_op | source)
XLA Modules:
  0.0 158.5 jit_solution(9165122495655938390)
XLA Ops:
  0.7 151.2 %encoder_layer.1 = (bf16[2,256,768]{2,1,0:T(8,128)(2,1)}, f32[256,768]{1,0:T(8,128)}, bf16[256,768]{1,0:T(8,128)(2,1)}, f32[16,768]{1,0:T(8,128)}, bf16[768,768]...) custom-call(bf16[256,2,768]{2,1,0:T(2,128)(2,1)} %refs_0_.1, bf16[256,2,768]{2,1,0:T(2,128)(2,1)} %refs_1_.1, ...), custom_call_target="tpu_custom_call" | custom-call | tf_op jit(solution)/shard_map/encoder_layer/pallas_call | solution.py:997
  151.9 6.4 %finish.1 = (f32[768,768]{1,0:T(8,128)}, f32[768,768]{1,0:T(8,128)}, f32[256,2,768]{2,1,0:T(2,128)}, bf16[256,2,768]{2,1,0:T(2,128)(2,1)}, f32[192,768]{1,0:T(8,...) custom-call(bf16[2,256,768]{2,1,0:T(8,128)(2,1)} %get-tuple-element., ...), custom_call_target="tpu_custom_call" | custom-call | tf_op jit(solution)/shard_map/finish/pallas_call | solution.py:1022
where the time goes:
time: 159 us
  Pallas kernels  158 us (99%)
    pallas_call x1, Pallas kernels, local(): pl.pallas_call(functools.partial(layer, plan, names), out_shape=[s for _,...  151 us
    pallas_call x1, Pallas kernels, local(): pl.pallas_call(functools.partial(finish, labels), in_specs=[hbm] * len(in...  6.43 us

commit v1 on v0

--- a/solution.py
+++ b/solution.py
@@ -255,7 +255,7 @@
         n = r[name].shape[0] // parts
         return k * n // of, n // of, n
 
-    def weight_x(name, k, of):
+    def weight_x(name, k, of, piece=piece):
         start, size, step_rows = cut(name, k, of)
         src = r[("wq", "wk", "wv", "wo")[k]] if name == "wa" else r[name]
         off = mult(piece * step_rows, 16)
@@ -272,19 +272,28 @@
         if gbits < 2:
             return []
         start, size, step_rows = cut(name, k, of)
-        b = k % 2
-        o = 1 - b
-        from_piece = piece + (1 << o) * (1 - 2 * bit[o])
-        at = pl.ds(mult(from_piece * step_rows + start, 16), size)
-        dst = r["W" + name].at[ox, at]
-        return [prepare(dst, dst, b)]
+        if name == "wd" and k == 1:
+            return []
+        ways = [(k % 2, start, size)]
+        if name == "wd":
+            low = size // 2 // 16 * 16
+            ways = [(0, start, low), (1, start + low, size - low)]
+        copies = []
+        for b, start, size in ways:
+            o = 1 - b
+            from_piece = piece + (1 << o) * (1 - 2 * bit[o])
+            at = pl.ds(mult(from_piece * step_rows + start, 16), size)
+            dst = r["W" + name].at[ox, at]
+            if size:
+                copies.append(prepare(dst, dst, b))
+        return copies
 
     def arrived(copies):
         for copy in copies:
             copy.wait_recv()
 
     half = block // 2
-    wa_x = [weight_x("wa", k, 4) for k in range(4)]
+    wa_x = [weight_x("wa", k, 4) for k in range(3)]
     b_x = [send(r[n], r["O" + n], "x") for n in ("bq", "bv", "bu")]
 
     def divide(ref):
@@ -300,7 +309,9 @@
     for k in range(2):
         src = r["XO"].at[pl.ds(k * half, half)]
         x_x.append(send(src, xs.at[pl.ds(own0 + mine + k * half, half)], "x"))
+    wa_x.append(weight_x("wa", 3, 4))
     late_x = {(name, k): weight_x(name, k, 2) for name in ("wu", "wd") for k in range(2)}
+    wd_far = [weight_x("wd", 1, 2, parts - 1 - piece)] if gbits == 2 else []
     x_c = [send(xs.at[at_mine], xs.at[at_mine], "c")]
     local_c.wait()
     own_rows, far_rows = divide(r["CI"])
@@ -328,7 +339,7 @@
     def project(s, first):
         i = lax.div(first, block)
         at = pl.ds(pl.multiple_of(first, block), block)
-        y = dnt(xs[at, :], r["Wwa"][s, : plan.qkv_cols, :]) + bias[s, 0:1, : plan.qkv_cols]
+        y = dnt(xs[at, :], r["Wwa"][s, : 3 * hc, :]) + bias[s, 0:1, : 3 * hc]
         slot0 = first + block * jnp.where(i == 1, 1, 0) - block * jnp.where(i == 2, 1, 0)
         slot = slot0 + lax.broadcasted_iota(jnp.int32, (block, 128), 0)
         masked = jnp.where(slot < valid, 0.0, NEG)
@@ -342,6 +353,8 @@
                 tile = y[:, unit // 2 * 128 : unit // 2 * 128 + 128]
                 if unit % 2:
                     tile = pltpu.roll(tile, 64, 1)
+                elif unit + 1 == 3 * heads:
+                    tile = jnp.concatenate([tile, end[:, HEAD_DIM:]], 1)
                 if k == 0:
                     tile = tile * SCALE
                 r[name][s * heads + h, at, :] = jnp.where(real, tile, end).astype(BF16)
@@ -357,26 +370,29 @@
     for copy in local_a:
         copy.wait()
     wa_h, wa_f = [], []
-    for k in range(4):
+    project(x, frames_at(0, mine))
+    for k in range(3):
         wa_x[k].wait_recv()
         wa_h.append(started(weight_hop("wa", k, 4)))
-    for k in range(4):
+    x_c.pop(0).wait_recv()
+    project(x, frames_at(1, mine))
+    for k in range(3):
         arrived(wa_h[k])
         wa_f += started(weight_far("wa", k, 4))
     arrived(b_x)
     set_bias(ox, r["Obq"], r["Obv"], r["Obu"])
-    x_x[0].wait_recv()
-    at_other = [pl.ds(own0 + other + k * half, half) for k in range(2)]
-    x_c.append(send(xs.at[at_other[0]], xs.at[at_other[0]], "c"))
-    x_c.pop(0).wait_recv()
+    for k in range(2):
+        x_x[k].wait_recv()
+        at_other = pl.ds(own0 + other + k * half, half)
+        x_c.append(send(xs.at[at_other], xs.at[at_other], "c"))
     arrived(wa_f)
-
-    @pl.loop(0, 4)
+    for copy in local_w:
+        copy.wait()
+
+    @pl.loop(0, 2)
     def _(i):
-        project(lax.rem(i, 2), frames_at(lax.div(i, 2), mine))
-
-    x_x[1].wait_recv()
-    x_c.append(send(xs.at[at_other[1]], xs.at[at_other[1]], "c"))
+        project(ox, frames_at(i, mine))
+
     for k in range(2):
         if k:
             arrived(x_c)
@@ -385,8 +401,9 @@
         def _(s, k=k):
             project(s, frames_at(k, other))
 
-    for copy in local_w:
-        copy.wait()
+    wa_x[3].wait_recv()
+    wo_h = started(weight_hop("wa", 3, 4))
+    wo_f = weight_far("wa", 3, 4)
 
     row_tiles = [slice(i * block, (i + 1) * block) for i in range(4)]
 
@@ -416,7 +433,11 @@
         arrived(late_h[name, k])
         started(late_f[name, k])
 
-    progress = [(1, hop, "wu", 1), (2, far, "wu", 0), (3, hop, "wd", 0)]
+    def far_out(name, k):
+        arrived(wo_h)
+        started(wo_f)
+
+    progress = [(1, far_out, "wa", 3), (1, hop, "wu", 1), (2, far, "wu", 0), (3, hop, "wd", 0)]
     progress += [(4, far, "wu", 1), (5, hop, "wd", 1)]
     hop("wu", 0)
 
@@ -488,6 +509,7 @@
         at = pl.ds(at0, block)
         return sum(dn(r["C"][s, at, :hc], r["Wwa"][s, 3 * hc :, :]) for s in range(2))
 
+    arrived(wo_f)
     ex = exchange(attn_out)
     hb_base, hb_c = shared(r["HB"])
 
@@ -514,10 +536,9 @@
             r["G"][s, at, :] = (u * cdf).astype(BF16)
             r["SL"][s, at, :] = u.astype(BF16)
 
+    up(x, 0, 2)
     far("wd", 0)
-    up(x, 0, 2)
     arrived(hb_c)
-    far("wd", 1)
     up(x, 2, 4)
     arrived(late_f["wu", 0] + late_f["wu", 1])
     up(ox, 0, 4)
@@ -526,7 +547,7 @@
         at = pl.ds(at0, block)
         return dn(r["G"][0, at, :], r["Wwd"][0]) + dn(r["G"][1, at, :], r["Wwd"][1])
 
-    arrived(late_f["wd", 0] + late_f["wd", 1])
+    arrived(late_h["wd", 1] + late_f["wd", 0] + wd_far)
     ex = exchange(ffn_out)
     df_base, df_c = shared(r["DF"])
     c_x.wait_recv()
@@ -561,8 +582,7 @@
         @pl.loop(0, n // size)
         def _(i):
             at = pl.ds(mult(row0 + i * size), size)
-            got = src[sd, pl.ds(mult(i * size), size), :].astype(F32)
-            dst[d, at, :] = (dst[d, at, :].astype(F32) + got).astype(BF16)
+            dst[d, at, :] = dst[d, at, :] + src[sd, pl.ds(mult(i * size), size), :]
 
     def stream(key):
         name, row0, n, order = plan.streams[key]

time: 159 us -> 155 us (0.975)
  Pallas kernels: 158 us -> 154 us
    pallas_call x1, Pallas kernels: 151 us -> 148 us  [local(): pl.pallas_call(functools.partial(layer, plan, names), out_shape=[s for _,...]
where the time goes in v1:
time: 155 us
  Pallas kernels  154 us (99%)
    pallas_call x1, Pallas kernels, local(): pl.pallas_call(functools.partial(layer, plan, names), out_shape=[s for _,...  148 us
    pallas_call x1, Pallas kernels, local(): pl.pallas_call(functools.partial(finish, labels), in_specs=[hbm] * len(in...  6.43 us

profile of v1, /device:TPU:0, one launch (start us, length us, event | category | flops | bytes accessed | tf_op | source)
XLA Modules:
  0.0 155.1 jit_solution(9177585268523737155)
XLA Ops:
  0.7 147.8 %encoder_layer.1 = (bf16[2,256,768]{2,1,0:T(8,128)(2,1)}, f32[256,768]{1,0:T(8,128)}, bf16[256,768]{1,0:T(8,128)(2,1)}, f32[16,768]{1,0:T(8,128)}, bf16[768,768]...) custom-call(bf16[256,2,768]{2,1,0:T(2,128)(2,1)} %refs_0_.1, bf16[256,2,768]{2,1,0:T(2,128)(2,1)} %refs_1_.1, ...), custom_call_target="tpu_custom_call" | custom-call | tf_op jit(solution)/shard_map/encoder_layer/pallas_call | solution.py:1017
  148.5 6.4 %finish.1 = (f32[768,768]{1,0:T(8,128)}, f32[768,768]{1,0:T(8,128)}, f32[256,2,768]{2,1,0:T(2,128)}, bf16[256,2,768]{2,1,0:T(2,128)(2,1)}, f32[192,768]{1,0:T(8,...) custom-call(bf16[2,256,768]{2,1,0:T(8,128)(2,1)} %get-tuple-element., ...), custom_call_target="tpu_custom_call" | custom-call | tf_op jit(solution)/shard_map/finish/pallas_call | solution.py:1042

commit v2 on v1

--- a/solution.py
+++ b/solution.py
@@ -528,9 +528,9 @@
     left(ex)
 
     def up(s, first, last):
-        @pl.loop(first, last)
+        @pl.loop(first // 2, last // 2)
         def _(i):
-            at = pl.ds(row(i), block)
+            at = pl.ds(pl.multiple_of(row(2 * i), own), own)
             u = dn(r["HB"][at, :], r["Wwu"][s]) + bias[s, 1:2, :ff]
             cdf = 0.5 * (1.0 + lax.erf(u * ROOT_HALF))
             r["G"][s, at, :] = (u * cdf).astype(BF16)
@@ -672,9 +672,9 @@
         @pl.loop(first, last)
         def _(i):
             at = pl.ds(row(i), block)
-            for s in range(2):
-                da = dnt(r["DF"][at, :], r["Wwd"][s])
-                u = r["SL"][s, at, :].astype(F32)
+            grads = [dnt(r["DF"][at, :], r["Wwd"][s]) for s in range(2)]
+            ups = [r["SL"][s, at, :].astype(F32) for s in range(2)]
+            for s, (da, u) in enumerate(zip(grads, ups)):
                 cdf = 0.5 * (1.0 + lax.erf(u * ROOT_HALF))
                 du = da * (cdf + u * (DENSITY * jnp.exp(-0.5 * u * u)))
                 add_sum(8 + s, col_sum(du))
@@ -692,10 +692,10 @@
             for k in range(4):
                 step((name, "os"[k % 2], k // 2), q == k)
 
-    slope(0, 2)
+    slope(0, 1)
     arrived(df_c)
     weight_grad("down", lambda s, at: r["G"][s, :, at], lambda s: r["DF"][...])
-    slope(2, 4)
+    slope(1, 4)
     step("slope")
     weight_grad("up", lambda s, at: r["HB"][:, at], lambda s: r["SL"][s])
 
@@ -826,10 +826,11 @@
 
     step("dx1")
     step("tail")
-    r["vec"][...] = sums[...]
+    vec_l = local(sums, r["vec"])
     out_x.wait_recv()
     dx_x.wait_recv()
     out_l.wait()
+    vec_l.wait()
     dx_l.wait()
     for copy in pending:
         copy.wait_send()
@@ -850,16 +851,32 @@
     hc = r["g_query"].shape[0]
     targets = {"F_down": ["g_down"], "F_up": ["g_up"]}
     targets["F_attn"] = ["g_query", "g_key", "g_value", "g_out"]
-    got = {}
+    got = {"vec": copy(r["vec"], r["i_vec"])}
     for n in targets:
         rows = r[n].shape[0] // 4
         for k in range(4):
             at = pl.ds(k * rows, rows)
             got[n, k] = copy(r[n].at[at], r["i_" + n].at[at])
-    for n in ("dx_own", "dx_far", "out", "vec"):
+    for n in ("dx_own", "dx_far", "out"):
         got[n] = copy(r[n], r["i_" + n])
     loads = len(used)
+
+    def vectors():
+        vec = r["i_vec"]
+        width, ff = r["s_bo"].shape[0], r["s_bu"].shape[0]
+        got["vec"].wait()
+        for k, n in enumerate(("bo", "g1", "c1", "bd", "g2", "c2")):
+            r["t_" + n][...] = vec[k, :width]
+        r["t_bu"][...] = jnp.where(first, vec[8, :ff], vec[9, :ff])
+        b3 = jnp.where(first, vec[10:11, :], vec[11:12, :])
+        r["t_bq"][...] = b3[:, :hc].reshape(hc)
+        r["t_bv"][...] = b3[:, 2 * hc : 3 * hc].reshape(hc)
+        for n in ("bo", "g1", "c1", "bd", "g2", "c2", "bu", "bq", "bv"):
+            copy(r["t_" + n], r["s_" + n])
+
     for n, outs in targets.items():
+        if n == "F_up":
+            vectors()
         rows = r[n].shape[0] // 4
         if len(outs) > 1:
             for k in range(4):
@@ -881,16 +898,6 @@
     for k in range(2):
         r["o_rows"][:, k, :] = r["i_out"][k]
     copy(r["o_rows"], r["rows"])
-    got["vec"].wait()
-    vec = r["i_vec"]
-    width = r["s_bo"].shape[0]
-    for k, n in enumerate(("bo", "g1", "c1", "bd", "g2", "c2")):
-        r["s_" + n][...] = vec[k, :width]
-    ff = r["s_bu"].shape[0]
-    r["s_bu"][...] = jnp.where(first, vec[8, :ff], vec[9, :ff])
-    b3 = jnp.where(first, vec[10:11, :], vec[11:12, :])
-    r["s_bq"][...] = b3[:, :hc].reshape(hc)
-    r["s_bv"][...] = b3[:, 2 * hc : 3 * hc].reshape(hc)
     for made in used[loads:]:
         made.wait()
 
@@ -950,7 +957,7 @@
         ("out", shape_of((2, block, width), BF16), hbm),
         ("dx_own", shape_of((block, width), F32), hbm),
         ("dx_far", shape_of((block, width), BF16), hbm),
-        ("vec", shape_of((16, wide), F32), vmem),
+        ("vec", shape_of((16, wide), F32), hbm),
     ]
     grads = (
         ("down", ff, width),
@@ -1036,16 +1043,17 @@
     small += [("s_bu", (ff,)), ("s_bq", (hc,)), ("s_bv", (hc,))]
     buffers = [("i_" + n, a.shape, a.dtype) for n, a in zip(inner_names, inner)]
     buffers += [("o_rows", frames, BF16), ("o_dx", frames, F32)]
+    buffers += [("t" + n[1:], shape, F32) for n, shape in small]
     buffers += [("o_" + n, got[n].shape, F32) for n in ("F_down", "F_up", "F_attn")]
     labels = inner_names + [n for n, _, _ in final] + [n for n, _ in small]
     labels += [n for n, _, _ in buffers] + ["sem"]
     results = pl.pallas_call(
         functools.partial(finish, labels),
         in_specs=[hbm] * len(inner),
-        out_specs=[hbm] * len(final) + [vmem] * len(small),
+        out_specs=[hbm] * (len(final) + len(small)),
         out_shape=[shape_of(n, t) for _, n, t in final] + [shape_of(n, F32) for _, n in small],
         scratch_shapes=[pltpu.VMEM(n, t) for _, n, t in buffers]
-        + [pltpu.SemaphoreType.DMA((32,))],
+        + [pltpu.SemaphoreType.DMA((64,))],
         compiler_params=pltpu.CompilerParams(vmem_limit_bytes=60 * 2**20),
         name="finish",
     )(*inner)

time: 155 us -> 154 us (level)
  no operation moved by 1% of the time
where the time goes in v2:
time: 154 us
  Pallas kernels  153 us (99%)
    pallas_call x1, Pallas kernels, local(): pl.pallas_call(functools.partial(layer, plan, names), out_shape=[s for _,...  147 us
    pallas_call x1, Pallas kernels, local(): pl.pallas_call(functools.partial(finish, labels), in_specs=[hbm] * len(in...  6.1 us

profile of v2, /device:TPU:0, one launch (start us, length us, event | category | flops | bytes accessed | tf_op | source)
XLA Modules:
  0.0 154.2 jit_solution(7067319779631404482)
XLA Ops:
  0.7 147.3 %encoder_layer.1 = (bf16[2,256,768]{2,1,0:T(8,128)(2,1)}, f32[256,768]{1,0:T(8,128)}, bf16[256,768]{1,0:T(8,128)(2,1)}, f32[16,768]{1,0:T(8,128)}, bf16[768,768]...) custom-call(bf16[256,2,768]{2,1,0:T(2,128)(2,1)} %refs_0_.1, bf16[256,2,768]{2,1,0:T(2,128)(2,1)} %refs_1_.1, ...), custom_call_target="tpu_custom_call" | custom-call | tf_op jit(solution)/shard_map/encoder_layer/pallas_call | solution.py:1024
  147.9 6.1 %finish.1 = (f32[768,768]{1,0:T(8,128)}, f32[768,768]{1,0:T(8,128)}, f32[256,2,768]{2,1,0:T(2,128)}, bf16[256,2,768]{2,1,0:T(2,128)(2,1)}, f32[192,768]{1,0:T(8,...) custom-call(bf16[2,256,768]{2,1,0:T(8,128)(2,1)} %get-tuple-element., ...), custom_call_target="tpu_custom_call" | custom-call | tf_op jit(solution)/shard_map/finish/pallas_call | solution.py:1050

commit v3 on v2

--- a/solution.py
+++ b/solution.py
@@ -475,6 +475,7 @@
 
         @pl.loop(0, 2)
         def _(i):
+            i = lax.rem(ox + i, 2)
             sbuf[i] = partial(row(2 + i)).astype(BF16)
             remote(sbuf.at[i], rbuf.at[i], base + i, "c").start()
 
@@ -515,6 +516,7 @@
 
     @pl.loop(0, 2)
     def _(i):
+        i = lax.rem(ox + i, 2)
         a = attn_out(row(i)) + rep[0:1, :width]
         z = xs[pl.ds(row(i), block), :].astype(F32) + a + received(ex, i)
         z = z - mean(z)
@@ -549,11 +551,13 @@
 
     arrived(late_h["wd", 1] + late_f["wd", 0] + wd_far)
     ex = exchange(ffn_out)
+    out_x = prepare(r["OB"].at[pl.ds(other, block)], r["out"].at[x], "x")
     df_base, df_c = shared(r["DF"])
     c_x.wait_recv()
 
     @pl.loop(0, 2)
-    def _(i):
+    def _(step_):
+        i = lax.rem(ox + step_, 2)
         at = pl.ds(pl.multiple_of(i * block, block), block)
         hidden = r["N1"][at, :] * rep[1:2, :width] + rep[2:3, :width]
         f = ffn_out(row(i)) + rep[3:4, :width]
@@ -562,6 +566,7 @@
         inv = lax.rsqrt(mean(z * z) + EPS)
         n2 = z * inv
         r["OB"][at, :] = (n2 * rep[4:5, :width] + rep[5:6, :width]).astype(BF16)
+        pl.when(step_ == 0)(out_x.start)
         dy = r["CT"][at, :].astype(F32)
         add_sum(4, col_sum(dy * n2))
         add_sum(5, col_sum(dy))
@@ -573,7 +578,6 @@
         r["DF"][pl.ds(row(i), block), :] = df
         share(r["DF"], df_base, i).start()
     left(ex)
-    out_x = send(r["OB"].at[pl.ds(other, block)], r["out"].at[x], "x")
     out_l = local(r["OB"].at[pl.ds(mine, block)], r["out"].at[x])
 
     def adder(dst, d, row0, src, sd, n):
@@ -709,6 +713,7 @@
 
     @pl.loop(0, 2)
     def _(i):
+        i = lax.rem(ox + i, 2)
         at = pl.ds(pl.multiple_of(i * block, block), block)
         dh = r["DZ"][at, :] + hidden_back(row(i))
         dh = dh + received(ex, i)
@@ -815,6 +820,7 @@
 
     @pl.loop(0, 2)
     def _(i):
+        i = lax.rem(ox + i, 2)
         at = pl.ds(pl.multiple_of(i * block, block), block)
         dx = r["DZ"][at, :] + input_back(row(i))
         r["DZ"][at, :] = dx + received(ex, i)

time: 154 us -> 155 us (level)
  no operation moved by 1% of the time
where the time goes in v3:
time: 155 us
  Pallas kernels  154 us (99%)
    pallas_call x1, Pallas kernels, local(): pl.pallas_call(functools.partial(layer, plan, names), out_shape=[s for _,...  148 us
    pallas_call x1, Pallas kernels, local(): pl.pallas_call(functools.partial(finish, labels), in_specs=[hbm] * len(in...  6.1 us

profile of v3, /device:TPU:0, one launch (start us, length us, event | category | flops | bytes accessed | tf_op | source)
XLA Modules:
  0.0 154.7 jit_solution(17494166473525113741)
XLA Ops:
  0.7 147.7 %encoder_layer.1 = (bf16[2,256,768]{2,1,0:T(8,128)(2,1)}, f32[256,768]{1,0:T(8,128)}, bf16[256,768]{1,0:T(8,128)(2,1)}, f32[16,768]{1,0:T(8,128)}, bf16[768,768]...) custom-call(bf16[256,2,768]{2,1,0:T(2,128)(2,1)} %refs_0_.1, bf16[256,2,768]{2,1,0:T(2,128)(2,1)} %refs_1_.1, ...), custom_call_target="tpu_custom_call" | custom-call | tf_op jit(solution)/shard_map/encoder_layer/pallas_call | solution.py:1030
  148.4 6.1 %finish.1 = (f32[768,768]{1,0:T(8,128)}, f32[768,768]{1,0:T(8,128)}, f32[256,2,768]{2,1,0:T(2,128)}, bf16[256,2,768]{2,1,0:T(2,128)(2,1)}, f32[192,768]{1,0:T(8,...) custom-call(bf16[2,256,768]{2,1,0:T(8,128)(2,1)} %get-tuple-element., ...), custom_call_target="tpu_custom_call" | custom-call | tf_op jit(solution)/shard_map/finish/pallas_call | solution.py:1056
